TPU v7x, 256 devices: a whole 4x4x8 slice. The times are simulated.
256 devices in a mesh: line: 128 (over x, y, z), tm: 2 (over core).
Axes of the slice: x: 4, y: 4, z: 8, core: 2. Of those that a mesh axis runs over, the one named last changes fastest.
Arguments:
- signal: bfloat16 [4096, 8192], P('line', 'tm'), may hold values from -6 to 6
- cotangent: bfloat16 [4096, 8192], P('line', 'tm'), may hold values from -6 to 6
- bank: bfloat16 [16384, 512], P('line'), may hold values from -0.5 to 0.5
- lengths: int32 [4096], P('line'), may hold values from 1 to 512
- kernel_ids: int32 [4096], P('line'), may hold values from 0 to 16383, as said below
Outputs:
- filtered: bfloat16 [4096, 8192], P('line', 'tm')
- signal_grad: bfloat16 [4096, 8192], P('line', 'tm')
- bank_grad: float32 [16384, 512], P('line', 'tm')
Inputs may be any that keep to these rules, and one draw needn't show every extreme that they name: `kernel_ids`: row k of the bank is held by the device of index k // 128 along line. Among the 32 lines of one device, at most 2 use rows held by one owner, and some owner's rows are used by exactly 2 lines of every device.
All inputs are finite; a program needn't handle non-finite values.
Results may differ from a plain program's by a relative error of at most 0.0075.
Values may be sent and summed in bfloat16 or wider, within the bound.
A program may use at most 128 MiB of HBM per device.

v0:
```python
import math

import jax
import jax.numpy as jnp
import numpy as np
from jax import lax
from jax.sharding import PartitionSpec as P


def passed_along(value, axis, steps):
    count = lax.axis_size(axis)
    leading, last = (max(0, -steps), min(count, count - steps))
    return lax.ppermute(value, axis, [(source, source + steps) for source in range(leading, last)])


def band_index(block_len, shifts):
    offsets = np.arange(shifts + 1)[:, None, None] * block_len
    rows = np.arange(block_len)[None, :, None]
    cols = np.arange(block_len)[None, None, :]
    return (offsets + rows - cols + block_len - 1).astype(np.int32)


def group_pass(block_len, shifts, taps_len, kernel_part, signal_ext, cotan_ext, blocks_part):
    groups = kernel_part.shape[0]
    blocks = blocks_part.shape[1]
    table = band_index(block_len, shifts)
    padded = jnp.concatenate(
        [
            jnp.zeros((groups, block_len - 1), jnp.bfloat16),
            kernel_part,
            jnp.zeros((groups, block_len), jnp.bfloat16),
        ],
        axis=1,
    )
    bands = jnp.take(padded, jnp.asarray(table.reshape(-1)), axis=1).reshape(
        groups, shifts + 1, block_len, block_len
    )
    forward = jnp.zeros((groups, blocks, block_len), jnp.float32)
    backward = jnp.zeros((groups, blocks, block_len), jnp.float32)
    pieces = []
    for step in range(shifts + 1):
        band = bands[:, step]
        earlier = signal_ext[:, shifts - step : shifts - step + blocks]
        later = cotan_ext[:, step : step + blocks]
        forward = forward + jnp.einsum(
            "gij,gbj->gbi", band, earlier, preferred_element_type=jnp.float32
        )
        backward = backward + jnp.einsum(
            "gij,gbi->gbj", band, later, preferred_element_type=jnp.float32
        )
        pieces.append(
            jnp.einsum("gbi,gbj->gij", blocks_part, earlier, preferred_element_type=jnp.float32)
        )
    products = jnp.stack(pieces, axis=1).reshape(groups, -1)
    lag_pad = jnp.zeros((groups, taps_len + 2 * block_len - 1), jnp.float32)
    lag_pad = lag_pad.at[:, jnp.asarray(table.reshape(-1))].add(products)
    lagged = lag_pad[:, block_len - 1 : block_len - 1 + taps_len]
    return (forward.reshape(groups, -1), backward.reshape(groups, -1), lagged)


def body(signal, cotangent, bank, lengths, kernel_ids):
    line_count, samples = signal.shape
    slot_total, taps_len = bank.shape
    owners = lax.axis_size("line")
    slot_count = max(2, 2 * line_count // owners)
    block_len = min(128, taps_len)
    holder = kernel_ids // slot_total
    inside = kernel_ids % slot_total
    places = jnp.arange(line_count)
    earlier = (holder[:, None] == holder[None, :]) & (places[None, :] < places[:, None])
    rank_of = jnp.sum(earlier.astype(jnp.int32), axis=1)
    chosen = (holder[None, None, :] == jnp.arange(owners)[:, None, None]) & (
        rank_of[None, None, :] == jnp.arange(slot_count)[None, :, None]
    )
    requests = jnp.sum(jnp.where(chosen, inside[None, None, :], 0), axis=2)
    asked_rows = lax.all_to_all(requests, "line", split_axis=0, concat_axis=0, tiled=True)
    lookup = (asked_rows[:, :, None] == jnp.arange(slot_total)[None, None, :]).astype(jnp.bfloat16)
    rows_out = jnp.einsum("sck,kt->sct", lookup, bank, preferred_element_type=jnp.float32).astype(
        jnp.bfloat16
    )
    fetched = lax.all_to_all(rows_out, "line", split_axis=0, concat_axis=0, tiled=True)
    picker = chosen.reshape(owners * slot_count, line_count)
    gathered = jnp.einsum(
        "rl,rt->lt",
        picker.astype(jnp.bfloat16),
        fetched.reshape(owners * slot_count, taps_len),
        preferred_element_type=jnp.float32,
    )
    tap_mask = jnp.arange(taps_len)[None, :] < lengths[:, None]
    kernels = jnp.where(tap_mask, gathered, 0.0).astype(jnp.bfloat16)
    tail_part = signal[:, samples - taps_len :]
    head_part = cotangent[:, :taps_len]
    prev_tail = passed_along(tail_part, "tm", 1)
    next_head = passed_along(head_part, "tm", -1)
    shifts = taps_len // block_len
    blocks = samples // block_len
    signal_ext = jnp.concatenate([prev_tail, signal], axis=1).reshape(
        line_count, blocks + shifts, block_len
    )
    cotan_ext = jnp.concatenate([cotangent, next_head], axis=1).reshape(
        line_count, blocks + shifts, block_len
    )
    cotan_blocks = cotangent.reshape(line_count, blocks, block_len)
    group_size = min(32, line_count)
    group_count = line_count // group_size

    def split_rows(array):
        return array.reshape((group_count, group_size) + array.shape[1:])

    def per_group(group_item):
        kernel_part, signal_part, cotan_part, blocks_part = group_item
        return group_pass(
            block_len, shifts, taps_len, kernel_part, signal_part, cotan_part, blocks_part
        )

    forward, backward, lagged = lax.map(
        per_group,
        (
            split_rows(kernels),
            split_rows(signal_ext),
            split_rows(cotan_ext),
            split_rows(cotan_blocks),
        ),
    )
    filtered = forward.reshape(line_count, samples).astype(jnp.bfloat16)
    signal_grad = backward.reshape(line_count, samples).astype(jnp.bfloat16)
    grad_scale = 1.0 / math.sqrt(samples * lax.axis_size("tm"))
    shares = jnp.where(tap_mask, lagged.reshape(line_count, taps_len), 0.0) * grad_scale
    half_taps = taps_len // lax.axis_size("tm")
    whole_sum = lax.psum(shares.astype(jnp.bfloat16), "tm").astype(jnp.float32)
    outgoing = lax.dynamic_slice_in_dim(whole_sum, lax.axis_index("tm") * half_taps, half_taps, 1)
    packed = jnp.einsum(
        "rl,lt->rt", picker.astype(jnp.float32), outgoing, precision=lax.Precision.HIGHEST
    ).reshape(owners, slot_count, -1)
    returned = lax.all_to_all(
        packed.astype(jnp.bfloat16), "line", split_axis=0, concat_axis=0, tiled=True
    ).astype(packed.dtype)
    owner_table = (asked_rows.reshape(-1)[:, None] == jnp.arange(slot_total)[None, :]).astype(
        jnp.float32
    )
    collected = jnp.einsum(
        "rk,rt->kt",
        owner_table,
        returned.reshape(owners * slot_count, -1),
        precision=lax.Precision.HIGHEST,
    )
    return (filtered, signal_grad, collected)


def solution(mesh):
    return jax.shard_map(
        body,
        mesh=mesh,
        in_specs=(P("line", "tm"), P("line", "tm"), P("line", None), P("line"), P("line")),
        out_specs=(P("line", "tm"), P("line", "tm"), P("line", "tm")),
        check_vma=False,
    )
```

profile of v0, /device:TPU:1, one launch (start us, length us, event | category | flops | bytes accessed | tf_op | source)
XLA Modules:
  0.0 903.9 jit_solution(13392449932072895999)
XLA Ops:
  1.4 1.3 collective-permute-start
  4.5 16.3 %all-to-all-start = ((s32[128,1,2]{2,1,0:T(1,128)}), s32[128,1,2]{2,1,0:T(1,128)S(1)}, u32[]{:S(2)}, u32[]{:S(2)}) async-start(s32[128,1,2]{2,1,0:T(1,128)} %copy.38), calls=%async_computation | async-start | bytes 131072 | tf_op jit(solution)/shard_map/all_to_all | solution.py:76
  21.6 3.3 collective-permute-start.1
  24.9 1.0 copy.67
  26.0 1.0 pad_maximum_fusion
  27.1 1.8 bitcast_dynamic-update-slice_fusion.4
  28.9 1.8 bitcast_dynamic-update-slice_fusion.3
  30.7 1.8 bitcast_dynamic-update-slice_fusion.2
  32.5 1.8 bitcast_dynamic-update-slice_fusion.1
  34.4 1.8 bitcast_dynamic-update-slice_fusion
  36.2 11.3 %copy.49 = f32[32,5,128,128]{3,2,1,0:T(8,128)} copy(f32[32,5,128,128]{2,3,0,1:T(8,128)} %bitcast_dynamic-update-slice_fusion) | data formatting | bytes 20971520 | tf_op jit(solution)/shard_map/while/body/eval_jaxpr/stack | solution.py:54
  47.5 14.0 %copy.74 = f32[4,8,640,128]{3,1,2,0:T(8,128)} copy(f32[4,8,640,128]{3,2,1,0:T(8,128)} %bitcast.84) | data formatting | bytes 20971520
  61.5 22.6 %copy.50 = f32[81920,32]{1,0:T(8,128)} copy(f32[81920,32]{0,1:T(8,128)} %bitcast.85) | data formatting | bytes 20971520 | tf_op jit(solution)/shard_map/while/body/eval_jaxpr/reshape | solution.py:54
  84.1 434.3 %scatter_custom_fusion = f32[32,767]{0,1:T(8,128)S(1)} fusion(s32[81920]{0:T(1024)S(1)} %copy-done.4, f32[81920,32]{1,0:T(8,128)} %copy.50, f32[]{:T(128)} %constant.82.clone.1), kind=kCustom, calls=%fused_computation.55 | custom fusion | flops 2621440 | bytes 98688 | tf_op jit(solution)/shard_map/while/body/eval_jaxpr/scatter-add | solution.py:56
  518.6 3.4 psum.7
  523.1 13.7 %all-to-all-start.2 = ((bf16[128,2,256]{2,1,0:T(2,128)(2,1)}), bf16[128,2,256]{2,1,0:T(2,128)(2,1)S(1)}, u32[]{:S(2)}, u32[]{:S(2)}) async-start(bf16[128,2,256]{2,1,0:T(2,128)(2,1)} %copy.52), calls=%async_computation.2 | async-start | bytes 262144 | tf_op jit(solution)/shard_map/all_to_all | solution.py:135
  537.3 1.0 copy.40
  539.8 8.5 all-to-all-done.2
  548.3 6.3 all-to-all-start.1
  555.8 11.6 %all-to-all-done.1 = bf16[128,2,512]{2,1,0:T(2,128)(2,1)S(1)} async-done(((bf16[128,2,512]{2,1,0:T(2,128)(2,1)}), bf16[128,2,512]{2,1,0:T(2,128)(2,1)S(1)}, u32[]{:S(2)}, u32[]{:S(2)}) %all-to-all-start.1) | async-done | bytes 262176 | tf_op jit(solution)/shard_map/all_to_all | solution.py:81
  567.9 286.0 %gather_fusion = bf16[81920,32]{1,0:T(8,128)(2,1)} fusion(bf16[32,767]{0,1:T(8,128)(2,1)S(1)} %copy.42, s32[81920]{0:T(1024)S(1)} %broadcast_clamp_fusion), kind=kCustom, calls=%fused_computation | custom fusion | bytes 10813440 | tf_op jit(solution)/shard_map/while/body/eval_jaxpr/jit(_take)/gather | solution.py:35
  853.9 15.2 %fusion.49 = (bf16[32,1,128,128]{0,3,2,1:T(8,128)(2,1)}, bf16[32,1,128,128]{0,3,2,1:T(8,128)(2,1)}, bf16[32,1,128,128]{0,3,2,1:T(8,128)(2,1)}, bf16[32,1,128,128]{0,3,2,1:T(8,128)(2,1)}, bf16[32,1,128,128]{0,3,2,1:T(8,128)(2,1)}) fusion(bf16[32,5,128,128]{0,3,2,1:T(8,128)(2,1)} %bitcast.86), kind=kLoop, calls=%fused_computation.88 | loop fusion | bytes 10485760 | tf_op jit(solution)/shard_map/while/body/eval_jaxpr/slice | solution.py:42
  869.1 4.0 copy.60
  873.1 1.5 fusion.12
  874.6 4.9 copy.59
  879.5 4.9 copy.61
  884.3 4.9 copy.62
  889.3 4.0 copy.63
  893.7 2.0 convolution_add_fusion.7
  895.7 1.6 convolution_add_fusion.3
  897.3 1.9 convolution_add_fusion.6
  899.2 1.6 convolution_add_fusion.2
  (52 shorter events, 11.9 us)
Async XLA Ops:
  0.6 536.4 %copy-start = (bf16[128,512]{1,0:T(8,128)(2,1)S(1)}, bf16[128,512]{1,0:T(8,128)(2,1)}, u32[]{:S(2)}) copy-start(bf16[128,512]{1,0:T(8,128)(2,1)} %param.9) | copy-start | bytes 393220
  1.4 24.5 %collective-permute-start = (bf16[32,512]{1,0:T(8,128)(2,1)S(1)}, bf16[32,512]{1,0:T(8,128)(2,1)S(1)}, u32[]{:S(2)}, u32[]{:S(2)}) collective-permute-start(bf16[32,512]{1,0:T(8,128)(2,1)S(1)} %slice.70), channel_id=1, source_target_pairs={{0,1},{2,3},{4,5},{6,7},{8,9},{10,11},{12,13},{14,15},{16,17},{18,... | collective-permute-start | bytes 98312 | tf_op jit(solution)/shard_map/ppermute | solution.py:13
  4.5 518.6 %all-to-all-start = ((s32[128,1,2]{2,1,0:T(1,128)}), s32[128,1,2]{2,1,0:T(1,128)S(1)}, u32[]{:S(2)}, u32[]{:S(2)}) async-start(s32[128,1,2]{2,1,0:T(1,128)} %copy.38), calls=%async_computation | async-start | bytes 131072 | tf_op jit(solution)/shard_map/all_to_all | solution.py:76
  21.6 533.0 %collective-permute-start.1 = (bf16[32,512]{1,0:T(8,128)(2,1)S(1)}, bf16[32,512]{1,0:T(8,128)(2,1)S(1)}, u32[]{:S(2)}, u32[]{:S(2)}) collective-permute-start(bf16[32,512]{1,0:T(8,128)(2,1)S(1)} %slice.81), channel_id=1, source_target_pairs={{1,0},{3,2},{5,4},{7,6},{9,8},{11,10},{13,12},{15,14},{17,16},{19,... | collective-permute-start | bytes 98312 | tf_op jit(solution)/shard_map/ppermute | solution.py:13
  61.5 22.6 %copy-start.4 = (s32[81920]{0:T(1024)S(1)}, s32[81920]{0:T(1024)}, u32[]{:S(2)}) copy-start(s32[81920]{0:T(1024)} %constant.102) | copy-start | bytes 983044
  61.5 457.0 %copy-start.5 = (s32[32]{0:T(128)S(1)}, s32[32]{0:T(128)}, u32[]{:S(2)}) copy-start(s32[32]{0:T(128)} %param.10) | copy-start | bytes 388
  61.5 493.2 %copy-start.3 = (bf16[32,4096]{1,0:T(8,128)(2,1)S(1)}, bf16[32,4096]{1,0:T(8,128)(2,1)}, u32[]{:S(2)}) copy-start(bf16[32,4096]{1,0:T(8,128)(2,1)} %param.8) | copy-start | bytes 786436
  523.1 25.2 %all-to-all-start.2 = ((bf16[128,2,256]{2,1,0:T(2,128)(2,1)}), bf16[128,2,256]{2,1,0:T(2,128)(2,1)S(1)}, u32[]{:S(2)}, u32[]{:S(2)}) async-start(bf16[128,2,256]{2,1,0:T(2,128)(2,1)} %copy.52), calls=%async_computation.2 | async-start | bytes 262144 | tf_op jit(solution)/shard_map/all_to_all | solution.py:135
  548.3 19.2 %all-to-all-start.1 = ((bf16[128,2,512]{2,1,0:T(2,128)(2,1)}), bf16[128,2,512]{2,1,0:T(2,128)(2,1)S(1)}, u32[]{:S(2)}, u32[]{:S(2)}) async-start(bf16[128,2,512]{2,1,0:T(2,128)(2,1)} %copy.40), calls=%async_computation.1 | async-start | bytes 524288 | tf_op jit(solution)/shard_map/all_to_all | solution.py:81
  889.3 14.6 %copy-start.1 = (bf16[128,512]{1,0:T(8,128)(2,1)S(1)}, bf16[128,512]{1,0:T(8,128)(2,1)}, u32[]{:S(2)}) copy-start(bf16[128,512]{1,0:T(8,128)(2,1)} %param.9) | copy-start | bytes 393220
  893.3 7.5 copy-start.2
where the time goes:
time: 906 us; the launch traced here: 904 us
  other arithmetic  437 us (48%)
  local copies, waits for them, and re-layouts  379 us (42%)
  starting transfers between devices  40.9 us (5%)
  matrix products  21.9 us (2%)
  waiting for transfers between devices  20.1 us (2%)
    scatter-add x1, other arithmetic, group_pass(): lag_pad = lag_pad.at[:, jnp.asarray(table.reshape(-1))].add(products)  434 us
    gather x1, local copies, waits for them, and re-layouts, group_pass(): jnp.take(padded, jnp.asarray(table.reshape(-1)), axis=1)  286 us
    unnamed x20, local copies, waits for them, and re-layouts  37.8 us
    reshape x1, local copies, waits for them, and re-layouts, group_pass(): products = jnp.stack(pieces, axis=1).reshape(groups, -1)  22.6 us
  transfers between devices with their start and end apart: 5, of which 2 were waited for; matrix products, arithmetic and copies ran while one was open for 55% of the time, Pallas kernels for 0%

commit v1 on v0

v1 whole, which is shorter than its diff:
```python
import math

import jax
import jax.numpy as jnp
from jax import lax
from jax.experimental import pallas as pl
from jax.experimental.pallas import tpu as pltpu
from jax.sharding import PartitionSpec as P

MESH = pl.DeviceIdType.MESH
BF = jnp.bfloat16
F32 = jnp.float32
LINES = 32
TAPS = 512
LANES = 128
SHIFTS = TAPS // LANES
SLOTS = 2
BANK_ROWS = 128


def iota(shape, dim):
    return lax.broadcasted_iota(jnp.int32, shape, dim)


def column(row):
    size = row.shape[1]
    mask = iota((size, size), 0) == iota((size, size), 1)
    return jnp.sum(jnp.where(mask, jnp.broadcast_to(row, (size, size)), 0.0), axis=1, keepdims=True)


def one_hot(hit):
    return jnp.where(hit, 1.0, 0.0)


def kernel(
    sig_hbm, cot_hbm, bank_hbm, len_ref, ids_ref,
    fil_hbm, grad_hbm, bgrad_hbm,
    sig, cot, bank, fil, grad, bgrad,
    halo, rq_out, rq_in, fe_out, fe_in, re_out, re_in,
    kx_out, kx_in, lx_out, lx_in, gx_out, gx_in,
    xf, cf, cjf, xjf, lhs, acc, kf, stage, owned, of, gf,
    in_sem, out_sem, halo_sem, rq_sem, fe_sem, re_sem, kx_sem, lx_sem, gx_sem,
):
    me = lax.axis_index("line")
    core = lax.axis_index("tm")
    other = (me, 1 - core)
    blocks = sig.shape[1] // LANES
    chips = rq_out.shape[0]
    par = lax.rem(me + core, 2)
    place = lax.div(me, 2)
    here_z = lax.rem(place, 4)
    here_y = lax.rem(lax.div(place, 4), 4)
    here_x = lax.div(place, 16)

    ins = [
        pltpu.make_async_copy(sig_hbm, sig, in_sem.at[0]),
        pltpu.make_async_copy(cot_hbm, cot, in_sem.at[1]),
        pltpu.make_async_copy(bank_hbm, bank, in_sem.at[2]),
    ]
    for copy in ins:
        copy.start()

    def peer(step):
        a = step // 16
        b = (step // 4) % 4
        c = step % 4
        z = lax.rem(here_z + 2 + (a * (a + 1)) // 2, 4)
        x = lax.rem(here_x + 2 + (b * (b + 1)) // 2, 4)
        y = lax.rem(here_y + 2 + (c * (c + 1)) // 2, 4)
        return x * 16 + y * 4 + z

    barrier = pltpu.get_barrier_semaphore()

    def greet(step, carry):
        pl.semaphore_signal(
            barrier, inc=1, device_id=(2 * peer(step) + par, core), device_id_type=MESH
        )
        return carry

    lax.fori_loop(0, chips - 1, greet, 0)

    @pl.when(core == 1)
    def _():
        pl.semaphore_signal(barrier, inc=1, device_id=(2 * place + par, core), device_id_type=MESH)

    pl.semaphore_signal(barrier, inc=1, device_id=other, device_id_type=MESH)

    def scatter(out_ref, in_ref, sems):
        def send(step, carry):
            i = peer(step)
            pltpu.make_async_remote_copy(
                src_ref=out_ref.at[i],
                dst_ref=in_ref.at[place],
                send_sem=sems.at[0],
                recv_sem=sems.at[1],
                device_id=(2 * i + par, core),
                device_id_type=MESH,
            ).start()
            return carry

        lax.fori_loop(0, chips - 1, send, 0)

        @pl.when(core == 1)
        def _():
            pltpu.make_async_remote_copy(
                src_ref=out_ref.at[place],
                dst_ref=in_ref.at[place],
                send_sem=sems.at[0],
                recv_sem=sems.at[1],
                device_id=(2 * place + par, core),
                device_id_type=MESH,
            ).start()

        @pl.when(core == 0)
        def _():
            pltpu.make_async_copy(out_ref.at[place], in_ref.at[place], sems.at[1]).start()

    def arrived(in_ref, sems):
        pltpu.make_async_copy(in_ref, in_ref, sems.at[1]).wait()

    def departed(out_ref, sems):
        part = out_ref.at[pl.ds(0, chips - 1)]
        pltpu.make_async_copy(part, part, sems.at[0]).wait()

        @pl.when(core == 1)
        def _():
            pltpu.make_async_copy(out_ref.at[0], out_ref.at[0], sems.at[0]).wait()

    def swap(out_ref, in_ref, sems):
        return pltpu.make_async_remote_copy(
            src_ref=out_ref,
            dst_ref=in_ref,
            send_sem=sems.at[0],
            recv_sem=sems.at[1],
            device_id=other,
            device_id_type=MESH,
        )

    ids_row = ids_ref[...].reshape(1, LINES)
    holder_row = ids_row // BANK_ROWS
    inside_row = ids_row % BANK_ROWS
    holder_col = column(holder_row.astype(F32)).astype(jnp.int32)
    inside_col = column(inside_row.astype(F32)).astype(jnp.int32)
    len_col = column(len_ref[...].reshape(1, LINES).astype(F32)).astype(jnp.int32)
    same = jnp.broadcast_to(holder_col, (LINES, LINES)) == jnp.broadcast_to(holder_row, (LINES, LINES))
    subs = iota((LINES, LINES), 0)
    lanes = iota((LINES, LINES), 1)
    rank_col = jnp.sum(one_hot(same & (lanes < subs)), axis=1, keepdims=True).astype(jnp.int32)
    rank_row = jnp.sum(one_hot(same & (subs < lanes)), axis=0, keepdims=True).astype(jnp.int32)
    spot_col = jnp.where(holder_col % 2 == par, holder_col // 2, -chips * SLOTS)
    spot_row = jnp.where(holder_row % 2 == par, holder_row // 2, -chips * SLOTS)
    picks = SLOTS * chips
    pick = one_hot(iota((LINES, picks), 1) == spot_col + rank_col * chips).astype(BF)
    pick_t = one_hot(iota((picks, LINES), 0) == spot_row + rank_row * chips).astype(BF)
    wanted = jnp.where(
        iota((chips, LINES), 0) == spot_row, (rank_row + 1).astype(F32), 0.0
    ).astype(BF)
    rows = one_hot(iota((LINES, BANK_ROWS), 1) == inside_col).astype(BF)
    asks = jnp.dot(wanted, rows, preferred_element_type=F32)
    rq_out[...] = asks.reshape(chips, 1, BANK_ROWS)
    tap_mask = iota((LINES, TAPS), 1) < len_col

    for copy in ins[:2]:
        copy.wait()
    pl.semaphore_wait(barrier, chips + core)

    scatter(rq_out, rq_in, rq_sem)

    @pl.when(core == 0)
    def _():
        swap(sig.at[:, pl.ds(blocks * LANES - TAPS, TAPS)], halo, halo_sem).start()

    @pl.when(core == 1)
    def _():
        swap(cot.at[:, pl.ds(0, TAPS)], halo, halo_sem).start()

    for q in range(blocks):
        span = slice(q * LANES, (q + 1) * LANES)
        xf[(SHIFTS + q) * LINES : (SHIFTS + q + 1) * LINES, :] = sig[:, span].astype(F32)
        cf[q * LINES : (q + 1) * LINES, :] = cot[:, span].astype(F32)
    pltpu.make_async_copy(halo, halo, halo_sem.at[1]).wait()
    for s in range(SHIFTS):
        edge = halo[:, s * LANES : (s + 1) * LANES].astype(F32)
        xf[s * LINES : (s + 1) * LINES, :] = jnp.where(core == 1, edge, 0.0)
        cf[(blocks + s) * LINES : (blocks + s + 1) * LINES, :] = jnp.where(core == 0, edge, 0.0)
    turn = one_hot(iota((LANES, LANES), 0) + iota((LANES, LANES), 1) == LANES - 1).astype(BF)
    flip_rows = 4 * LINES

    def flip(step, carry):
        at = pl.ds(pl.multiple_of(step * flip_rows, flip_rows), flip_rows)
        cjf[at, :] = jnp.dot(cf[at, :].astype(BF), turn, preferred_element_type=F32)
        at_x = pl.ds(pl.multiple_of(step * flip_rows + SHIFTS * LINES, flip_rows), flip_rows)
        xjf[at, :] = jnp.dot(xf[at_x, :].astype(BF), turn, preferred_element_type=F32)
        return carry

    lax.fori_loop(0, blocks // 4, flip, 0)
    last = slice(blocks * LINES, (blocks + SHIFTS) * LINES)
    cjf[last, :] = jnp.dot(cf[last, :].astype(BF), turn, preferred_element_type=F32)

    ins[2].wait()
    arrived(rq_in, rq_sem)
    asked = rq_in[...].reshape(chips, BANK_ROWS)
    first = one_hot((asked == 1.0) | (asked == 3.0))
    second = one_hot(asked >= 2.0)
    owned[...] = jnp.concatenate([first, second], axis=0).astype(BF)

    def pack_slots(values, out_ref):
        for slot in range(SLOTS):
            for s in range(SHIFTS):
                stage[pl.ds(slot * SHIFTS + s, chips, stride=SLOTS * SHIFTS), :] = values[
                    slot * chips : (slot + 1) * chips, s * LANES : (s + 1) * LANES
                ]
        out_ref[...] = stage[...].reshape(chips, SLOTS * SHIFTS, LANES).astype(BF)

    def unpack_slots(in_ref):
        stage[...] = in_ref[...].astype(F32).reshape(chips * SLOTS * SHIFTS, LANES)
        return jnp.concatenate(
            [
                jnp.concatenate(
                    [
                        stage[pl.ds(slot * SHIFTS + s, chips, stride=SLOTS * SHIFTS), :]
                        for s in range(SHIFTS)
                    ],
                    axis=1,
                )
                for slot in range(SLOTS)
            ],
            axis=0,
        ).astype(BF)

    pack_slots(jnp.dot(owned[...], bank[...], preferred_element_type=F32), fe_out)
    scatter(fe_out, fe_in, fe_sem)

    across = iota((LANES, LANES), 0) + iota((LANES, LANES), 1) >= LANES - 1

    def lag_line(line):
        here = xjf[pl.ds(line, blocks, stride=LINES), :].astype(BF)
        later = jnp.concatenate(
            [
                cf[pl.ds(s * LINES + line, blocks, stride=LINES), :].astype(BF)
                for s in range(SHIFTS + 1)
            ],
            axis=1,
        )
        prod = lax.dot_general(
            here, later, (((0,), (0,)), ((), ())), preferred_element_type=F32
        )
        for s in range(SHIFTS):
            part = jnp.where(
                across,
                prod[:, s * LANES : (s + 1) * LANES],
                prod[:, (s + 1) * LANES : (s + 2) * LANES],
            )
            part = pltpu.roll(part, 1, 1, stride=1, stride_axis=0)
            part = jnp.sum(part.reshape(LANES // 8, 8, LANES), axis=0)
            acc[s, pl.ds(pl.multiple_of(line * 8, 8), 8), :] = part

    def windows(line):
        for s in range(SHIFTS + 1):
            span = slice(s * LANES, (s + 1) * LANES)
            lhs[line, 0:blocks, span] = xf[
                pl.ds((SHIFTS - s) * LINES + line, blocks, stride=LINES), :
            ].astype(BF)
            lhs[line, blocks : 2 * blocks, span] = cjf[
                pl.ds(s * LINES + line, blocks, stride=LINES), :
            ].astype(BF)

    def before(step, carry):
        for u in range(2):
            lag_line(step * 2 + u)
            windows(step * 2 + u)
        return carry

    lax.fori_loop(0, LINES // 2, before, 0)
    scale = 1.0 / math.sqrt(2 * blocks * LANES)
    lag = jnp.concatenate(
        [
            sum(acc[s, pl.ds(r, LINES, stride=8), :] for r in range(8))
            for s in range(SHIFTS)
        ],
        axis=1,
    )
    lx_out[...] = jnp.where(tap_mask, lag, 0.0) * scale
    lag_swap = swap(lx_out, lx_in, lx_sem)
    lag_swap.start()
    lag_swap.wait_recv()
    lag = (lx_out[...] + lx_in[...]).astype(BF)
    pack_slots(jnp.dot(pick_t, lag, preferred_element_type=F32), re_out)
    scatter(re_out, re_in, re_sem)

    arrived(fe_in, fe_sem)
    mine = jnp.dot(pick, unpack_slots(fe_in), preferred_element_type=F32)
    kx_out[...] = jnp.where(tap_mask, mine, 0.0).astype(BF)
    tap_swap = swap(kx_out, kx_in, kx_sem)
    tap_swap.start()
    tap_swap.wait_recv()
    taps = kx_out[...].astype(F32) + kx_in[...].astype(F32)
    for s in range(SHIFTS):
        kf[s * LINES : (s + 1) * LINES, :] = taps[:, s * LANES : (s + 1) * LANES]

    upper = iota((LANES, LANES), 1) >= iota((LANES, LANES), 0)

    def filter_line(line):
        bands = []
        before_it = jnp.zeros((LANES, LANES), F32)
        for s in range(SHIFTS):
            row = kf[pl.ds(s * LINES + line, 1), :]
            rolled = pltpu.roll(
                jnp.broadcast_to(row, (LANES, LANES)), 0, 1, stride=1, stride_axis=0
            )
            bands.append(jnp.where(upper, rolled, before_it).astype(BF))
            before_it = rolled
        bands.append(jnp.where(upper, 0.0, before_it).astype(BF))
        both = jnp.dot(
            lhs[line], jnp.concatenate(bands, axis=0), preferred_element_type=F32
        )
        of[pl.ds(line, blocks, stride=LINES), :] = both[:blocks]
        gf[pl.ds(line, blocks, stride=LINES), :] = both[blocks:]

    def filters(half):
        def step_of(step, carry):
            for u in range(2):
                filter_line(half * 16 + step * 2 + u)
            return carry

        lax.fori_loop(0, 8, step_of, 0)
        copies = []
        at = slice(half * 16, half * 16 + 16)
        for q in range(blocks):
            span = slice(q * LANES, (q + 1) * LANES)
            from_ = slice(q * LINES + half * 16, q * LINES + half * 16 + 16)
            fil[at, span] = of[from_, :].astype(BF)
            grad[at, span] = jnp.dot(
                gf[from_, :].astype(BF), turn, preferred_element_type=F32
            ).astype(BF)
        copies = [
            pltpu.make_async_copy(fil.at[at], fil_hbm.at[at], out_sem.at[2 * half]),
            pltpu.make_async_copy(grad.at[at], grad_hbm.at[at], out_sem.at[2 * half + 1]),
        ]
        for copy in copies:
            copy.start()
        return copies

    outs = filters(0)

    arrived(re_in, re_sem)
    total = lax.dot_general(
        owned[...], unpack_slots(re_in), (((0,), (0,)), ((), ())), preferred_element_type=F32
    )
    half_taps = TAPS // 2
    gx_out[...] = jnp.where(core == 0, total[:, half_taps:], total[:, :half_taps])
    bgrad[...] = jnp.where(core == 0, total[:, :half_taps], total[:, half_taps:])
    sum_swap = swap(gx_out, gx_in, gx_sem)
    sum_swap.start()

    outs = outs + filters(1)
    sum_swap.wait_recv()
    bgrad[...] = bgrad[...] + gx_in[...]
    outs.append(pltpu.make_async_copy(bgrad, bgrad_hbm, out_sem.at[4]))
    outs[-1].start()

    pltpu.make_async_copy(halo, halo, halo_sem.at[0]).wait()
    departed(rq_out, rq_sem)
    departed(fe_out, fe_sem)
    departed(re_out, re_sem)
    lag_swap.wait_send()
    tap_swap.wait_send()
    sum_swap.wait_send()
    for copy in outs:
        copy.wait()


def body(signal, cotangent, bank, lengths, kernel_ids):
    line_count, samples = signal.shape
    blocks = samples // LANES
    chips = lax.axis_size("line") // 2
    any_ = pl.BlockSpec(memory_space=pl.ANY)
    vmem = pl.BlockSpec(memory_space=pltpu.VMEM)
    message = (chips, SLOTS * SHIFTS, LANES)
    pair = pltpu.SemaphoreType.DMA((2,))
    return pl.pallas_call(
        kernel,
        out_shape=(
            jax.ShapeDtypeStruct((line_count, samples), BF),
            jax.ShapeDtypeStruct((line_count, samples), BF),
            jax.ShapeDtypeStruct((BANK_ROWS, TAPS // 2), F32),
        ),
        in_specs=[any_, any_, any_, vmem, vmem],
        out_specs=(any_, any_, any_),
        scratch_shapes=[
            pltpu.VMEM((line_count, samples), BF),
            pltpu.VMEM((line_count, samples), BF),
            pltpu.VMEM((BANK_ROWS, TAPS), BF),
            pltpu.VMEM((line_count, samples), BF),
            pltpu.VMEM((line_count, samples), BF),
            pltpu.VMEM((BANK_ROWS, TAPS // 2), F32),
            pltpu.VMEM((line_count, TAPS), BF),
            pltpu.VMEM((chips, 1, LANES), F32),
            pltpu.VMEM((chips, 1, LANES), F32),
            pltpu.VMEM(message, BF),
            pltpu.VMEM(message, BF),
            pltpu.VMEM(message, BF),
            pltpu.VMEM(message, BF),
            pltpu.VMEM((line_count, TAPS), BF),
            pltpu.VMEM((line_count, TAPS), BF),
            pltpu.VMEM((line_count, TAPS), F32),
            pltpu.VMEM((line_count, TAPS), F32),
            pltpu.VMEM((BANK_ROWS, TAPS // 2), F32),
            pltpu.VMEM((BANK_ROWS, TAPS // 2), F32),
            pltpu.VMEM(((blocks + SHIFTS) * line_count, LANES), F32),
            pltpu.VMEM(((blocks + SHIFTS) * line_count, LANES), F32),
            pltpu.VMEM(((blocks + SHIFTS) * line_count, LANES), F32),
            pltpu.VMEM((blocks * line_count, LANES), F32),
            pltpu.VMEM((line_count, 2 * blocks, TAPS + LANES), BF),
            pltpu.VMEM((SHIFTS, 8 * line_count, LANES), F32),
            pltpu.VMEM((SHIFTS * line_count, LANES), F32),
            pltpu.VMEM((chips * SLOTS * SHIFTS, LANES), F32),
            pltpu.VMEM((SLOTS * chips, BANK_ROWS), BF),
            pltpu.VMEM((blocks * line_count, LANES), F32),
            pltpu.VMEM((blocks * line_count, LANES), F32),
            pltpu.SemaphoreType.DMA((3,)),
            pltpu.SemaphoreType.DMA((5,)),
            pair, pair, pair, pair, pair, pair, pair,
        ],
        compiler_params=pltpu.CompilerParams(
            collective_id=0, has_side_effects=True, vmem_limit_bytes=48 * 1024 * 1024
        ),
        cost_estimate=pl.CostEstimate(
            flops=6 * line_count * samples * TAPS, bytes_accessed=1 << 21, transcendentals=0
        ),
    )(signal, cotangent, bank, lengths, kernel_ids)


def solution(mesh):
    return jax.shard_map(
        body,
        mesh=mesh,
        in_specs=(P("line", "tm"), P("line", "tm"), P("line", None), P("line"), P("line")),
        out_specs=(P("line", "tm"), P("line", "tm"), P("line", "tm")),
        check_vma=False,
    )
```

time: 906 us -> 56.2 us (0.06)
  other arithmetic: 437 us -> 0 us
  local copies, waits for them, and re-layouts: 379 us -> 6.17 us
  Pallas kernels: 0 us -> 49.2 us
  starting transfers between devices: 40.9 us -> 0 us
  matrix products: 21.9 us -> 0 us
  waiting for transfers between devices: 20.1 us -> 0 us
    scatter-add x1 -> x0, other arithmetic: 434 us -> none  [group_pass(): lag_pad = lag_pad.at[:, jnp.asarray(table.reshape(-1))].add(products)]
    gather x1 -> x0, local copies, waits for them, and re-layouts: 286 us -> none  [group_pass(): jnp.take(padded, jnp.asarray(table.reshape(-1)), axis=1)]
    pallas_call x0 -> x1, Pallas kernels: none -> 49.2 us  [body(): pl.pallas_call(kernel, out_shape=(jax.ShapeDtypeStruct((line_count, sampl...]
    all_to_all x3 -> x0, starting transfers between devices: 36.4 us -> none  [the longest x1 16.3 us: body(): lax.all_to_all(requests, 'line', split_axis=0, concat_axis=0, tiled=True)]
    unnamed x20 -> x13, local copies, waits for them, and re-layouts: 37.8 us -> 6.17 us
    reshape x2 -> x0, local copies, waits for them, and re-layouts: 22.7 us -> none  [the longest x1 22.6 us: group_pass(): products = jnp.stack(pieces, axis=1).reshape(groups, -1)]
    dot_general x19 -> x0, matrix products: 21.9 us -> none  [the longest x5 9.07 us: group_pass(): jnp.einsum('gbi,gbj->gij', blocks_part, earlier, preferred_element_type=j...]
    all_to_all x3 -> x0, waiting for transfers between devices: 20.1 us -> none  [the longest x1 11.6 us: body(): lax.all_to_all(rows_out, 'line', split_axis=0, concat_axis=0, tiled=True)]
  transfers between devices with their start and end apart: 5 -> 0, of which waited for: 2 -> 0; matrix products, arithmetic and copies ran while one was open for 55% -> 0% of each run, Pallas kernels for 0% -> 0%
where the time goes in v1:
time: 56.2 us; the launch traced here: 56.1 us
  Pallas kernels  49.2 us (88%)
  local copies, waits for them, and re-layouts  6.17 us (11%)
  between operations  0.65 us (1%)
    pallas_call x1, Pallas kernels, body(): pl.pallas_call(kernel, out_shape=(jax.ShapeDtypeStruct((line_count, sampl...  49.2 us
    unnamed x13, local copies, waits for them, and re-layouts  6.17 us

profile of v1, /device:TPU:1, one launch (start us, length us, event | category | flops | bytes accessed | tf_op | source)
XLA Modules:
  0.0 56.1 jit_solution(9506285473690095727)
XLA Ops:
  0.6 0.0 copy-start
  0.6 0.9 %copy-done = bf16[32,4096]{1,0:T(8,128)(2,1)S(1)} copy-done((bf16[32,4096]{1,0:T(8,128)(2,1)S(1)}, bf16[32,4096]{1,0:T(8,128)(2,1)}, u32[]{:S(2)}) %copy-start) | copy-done | bytes 262168
  1.6 0.0 copy-start.1
  1.6 0.9 %copy-done.1 = bf16[32,4096]{1,0:T(8,128)(2,1)S(1)} copy-done((bf16[32,4096]{1,0:T(8,128)(2,1)S(1)}, bf16[32,4096]{1,0:T(8,128)(2,1)}, u32[]{:S(2)}) %copy-start.1) | copy-done | bytes 262168
  2.5 0.0 copy-start.2
  2.5 0.9 %copy-done.2 = bf16[128,512]{1,0:T(8,128)(2,1)S(1)} copy-done((bf16[128,512]{1,0:T(8,128)(2,1)S(1)}, bf16[128,512]{1,0:T(8,128)(2,1)}, u32[]{:S(2)}) %copy-start.2) | copy-done | bytes 131096
  3.4 0.0 copy-start.3
  3.4 0.7 %copy-done.3 = s32[32]{0:T(128)S(1)} copy-done((s32[32]{0:T(128)S(1)}, s32[32]{0:T(128)}, u32[]{:S(2)}) %copy-start.3) | copy-done | bytes 152
  4.1 0.0 copy-start.4
  4.1 0.7 %copy-done.4 = s32[32]{0:T(128)S(1)} copy-done((s32[32]{0:T(128)S(1)}, s32[32]{0:T(128)}, u32[]{:S(2)}) %copy-start.4) | copy-done | bytes 152
  4.7 49.2 %shard_map.76 = (bf16[32,4096]{1,0:T(8,128)(2,1)S(1)}, bf16[32,4096]{1,0:T(8,128)(2,1)S(1)}, f32[128,256]{1,0:T(8,128)S(1)}) custom-call(bf16[32,4096]{1,0:T(8,128)(2,1)S(1)} %copy-done, bf16[32,4096]{1,0:T(8,128)(2,1)S(1)} %copy-done.1, bf16[128,512]{1,0:T(8,128)(2,1)S(1)} %copy-done.2, s32[32]{0:T(128)S(1)} %copy-done.3, s32[32]{0:T(128)S(1)} %copy-done.4), custom_call_target="tpu_custom_call" | custom-call | flops 402653184 | bytes 2097152 | tf_op jit(solution)/shard_map/pallas_call | solution.py:381
  54.0 0.7 %copy.11 = bf16[32,4096]{1,0:T(8,128)(2,1)} copy(bf16[32,4096]{1,0:T(8,128)(2,1)S(1)} %get-tuple-element.6) | data formatting | bytes 524288
  54.7 0.7 %copy.12 = bf16[32,4096]{1,0:T(8,128)(2,1)} copy(bf16[32,4096]{1,0:T(8,128)(2,1)S(1)} %get-tuple-element.7) | data formatting | bytes 524288
  55.4 0.7 %copy.13 = f32[128,256]{1,0:T(8,128)} copy(f32[128,256]{1,0:T(8,128)S(1)} %get-tuple-element.8) | data formatting | bytes 262144
Async XLA Ops:
  0.6 1.0 %copy-start = (bf16[32,4096]{1,0:T(8,128)(2,1)S(1)}, bf16[32,4096]{1,0:T(8,128)(2,1)}, u32[]{:S(2)}) copy-start(bf16[32,4096]{1,0:T(8,128)(2,1)} %sig_hbm.1) | copy-start | bytes 786436
  1.6 0.9 %copy-start.1 = (bf16[32,4096]{1,0:T(8,128)(2,1)S(1)}, bf16[32,4096]{1,0:T(8,128)(2,1)}, u32[]{:S(2)}) copy-start(bf16[32,4096]{1,0:T(8,128)(2,1)} %cot_hbm.1) | copy-start | bytes 786436
  2.5 0.9 %copy-start.2 = (bf16[128,512]{1,0:T(8,128)(2,1)S(1)}, bf16[128,512]{1,0:T(8,128)(2,1)}, u32[]{:S(2)}) copy-start(bf16[128,512]{1,0:T(8,128)(2,1)} %bank_hbm.1) | copy-start | bytes 393220
  3.4 0.7 %copy-start.3 = (s32[32]{0:T(128)S(1)}, s32[32]{0:T(128)}, u32[]{:S(2)}) copy-start(s32[32]{0:T(128)} %len_ref.1) | copy-start | bytes 388
  4.1 0.7 %copy-start.4 = (s32[32]{0:T(128)S(1)}, s32[32]{0:T(128)}, u32[]{:S(2)}) copy-start(s32[32]{0:T(128)} %ids_ref.1) | copy-start | bytes 388

commit v2 on v1

--- a/solution.py
+++ b/solution.py
@@ -16,6 +16,7 @@
 SHIFTS = TAPS // LANES
 SLOTS = 2
 BANK_ROWS = 128
+PITCH = LINES + 1
 
 
 def iota(shape, dim):
@@ -33,13 +34,13 @@
 
 
 def kernel(
-    sig_hbm, cot_hbm, bank_hbm, len_ref, ids_ref,
-    fil_hbm, grad_hbm, bgrad_hbm,
-    sig, cot, bank, fil, grad, bgrad,
+    sig_hbm, cot_hbm, bank_hbm, len_hbm, ids_hbm,
+    fil, grad, bgrad,
+    sig, cot, bank, len_ref, ids_ref,
     halo, rq_out, rq_in, fe_out, fe_in, re_out, re_in,
     kx_out, kx_in, lx_out, lx_in, gx_out, gx_in,
     xf, cf, cjf, xjf, lhs, acc, kf, stage, owned, of, gf,
-    in_sem, out_sem, halo_sem, rq_sem, fe_sem, re_sem, kx_sem, lx_sem, gx_sem,
+    in_sem, halo_sem, rq_sem, fe_sem, re_sem, kx_sem, lx_sem, gx_sem,
 ):
     me = lax.axis_index("line")
     core = lax.axis_index("tm")
@@ -53,9 +54,11 @@
     here_x = lax.div(place, 16)
 
     ins = [
-        pltpu.make_async_copy(sig_hbm, sig, in_sem.at[0]),
-        pltpu.make_async_copy(cot_hbm, cot, in_sem.at[1]),
-        pltpu.make_async_copy(bank_hbm, bank, in_sem.at[2]),
+        pltpu.make_async_copy(ids_hbm, ids_ref, in_sem.at[0]),
+        pltpu.make_async_copy(len_hbm, len_ref, in_sem.at[1]),
+        pltpu.make_async_copy(sig_hbm, sig, in_sem.at[2]),
+        pltpu.make_async_copy(cot_hbm, cot, in_sem.at[3]),
+        pltpu.make_async_copy(bank_hbm, bank, in_sem.at[4]),
     ]
     for copy in ins:
         copy.start()
@@ -77,7 +80,7 @@
         )
         return carry
 
-    lax.fori_loop(0, chips - 1, greet, 0)
+    lax.fori_loop(0, chips - 1, greet, 0, unroll=9)
 
     @pl.when(core == 1)
     def _():
@@ -98,7 +101,7 @@
             ).start()
             return carry
 
-        lax.fori_loop(0, chips - 1, send, 0)
+        lax.fori_loop(0, chips - 1, send, 0, unroll=9)
 
         @pl.when(core == 1)
         def _():
@@ -136,6 +139,8 @@
             device_id_type=MESH,
         )
 
+    for copy in ins[:2]:
+        copy.wait()
     ids_row = ids_ref[...].reshape(1, LINES)
     holder_row = ids_row // BANK_ROWS
     inside_row = ids_row % BANK_ROWS
@@ -160,8 +165,16 @@
     rq_out[...] = asks.reshape(chips, 1, BANK_ROWS)
     tap_mask = iota((LINES, TAPS), 1) < len_col
 
-    for copy in ins[:2]:
+    for copy in ins[2:4]:
         copy.wait()
+    turn = one_hot(iota((LANES, LANES), 0) + iota((LANES, LANES), 1) == LANES - 1).astype(BF)
+    for q in range(blocks):
+        span = slice(q * LANES, (q + 1) * LANES)
+        at = slice(q * PITCH, q * PITCH + LINES)
+        xf[(SHIFTS + q) * PITCH : (SHIFTS + q) * PITCH + LINES, :] = sig[:, span].astype(F32)
+        cf[at, :] = cot[:, span].astype(F32)
+        xjf[at, :] = jnp.dot(sig[:, span], turn, preferred_element_type=F32)
+        cjf[at, :] = jnp.dot(cot[:, span], turn, preferred_element_type=F32)
     pl.semaphore_wait(barrier, chips + core)
 
     scatter(rq_out, rq_in, rq_sem)
@@ -174,70 +187,23 @@
     def _():
         swap(cot.at[:, pl.ds(0, TAPS)], halo, halo_sem).start()
 
-    for q in range(blocks):
-        span = slice(q * LANES, (q + 1) * LANES)
-        xf[(SHIFTS + q) * LINES : (SHIFTS + q + 1) * LINES, :] = sig[:, span].astype(F32)
-        cf[q * LINES : (q + 1) * LINES, :] = cot[:, span].astype(F32)
     pltpu.make_async_copy(halo, halo, halo_sem.at[1]).wait()
     for s in range(SHIFTS):
-        edge = halo[:, s * LANES : (s + 1) * LANES].astype(F32)
-        xf[s * LINES : (s + 1) * LINES, :] = jnp.where(core == 1, edge, 0.0)
-        cf[(blocks + s) * LINES : (blocks + s + 1) * LINES, :] = jnp.where(core == 0, edge, 0.0)
-    turn = one_hot(iota((LANES, LANES), 0) + iota((LANES, LANES), 1) == LANES - 1).astype(BF)
-    flip_rows = 4 * LINES
-
-    def flip(step, carry):
-        at = pl.ds(pl.multiple_of(step * flip_rows, flip_rows), flip_rows)
-        cjf[at, :] = jnp.dot(cf[at, :].astype(BF), turn, preferred_element_type=F32)
-        at_x = pl.ds(pl.multiple_of(step * flip_rows + SHIFTS * LINES, flip_rows), flip_rows)
-        xjf[at, :] = jnp.dot(xf[at_x, :].astype(BF), turn, preferred_element_type=F32)
-        return carry
-
-    lax.fori_loop(0, blocks // 4, flip, 0)
-    last = slice(blocks * LINES, (blocks + SHIFTS) * LINES)
-    cjf[last, :] = jnp.dot(cf[last, :].astype(BF), turn, preferred_element_type=F32)
-
-    ins[2].wait()
-    arrived(rq_in, rq_sem)
-    asked = rq_in[...].reshape(chips, BANK_ROWS)
-    first = one_hot((asked == 1.0) | (asked == 3.0))
-    second = one_hot(asked >= 2.0)
-    owned[...] = jnp.concatenate([first, second], axis=0).astype(BF)
-
-    def pack_slots(values, out_ref):
-        for slot in range(SLOTS):
-            for s in range(SHIFTS):
-                stage[pl.ds(slot * SHIFTS + s, chips, stride=SLOTS * SHIFTS), :] = values[
-                    slot * chips : (slot + 1) * chips, s * LANES : (s + 1) * LANES
-                ]
-        out_ref[...] = stage[...].reshape(chips, SLOTS * SHIFTS, LANES).astype(BF)
-
-    def unpack_slots(in_ref):
-        stage[...] = in_ref[...].astype(F32).reshape(chips * SLOTS * SHIFTS, LANES)
-        return jnp.concatenate(
-            [
-                jnp.concatenate(
-                    [
-                        stage[pl.ds(slot * SHIFTS + s, chips, stride=SLOTS * SHIFTS), :]
-                        for s in range(SHIFTS)
-                    ],
-                    axis=1,
-                )
-                for slot in range(SLOTS)
-            ],
-            axis=0,
-        ).astype(BF)
-
-    pack_slots(jnp.dot(owned[...], bank[...], preferred_element_type=F32), fe_out)
-    scatter(fe_out, fe_in, fe_sem)
+        edge = halo[:, s * LANES : (s + 1) * LANES]
+        before_it = jnp.where(core == 1, edge.astype(F32), 0.0)
+        after_it = jnp.where(core == 0, edge.astype(F32), 0.0)
+        at = slice((blocks + s) * PITCH, (blocks + s) * PITCH + LINES)
+        xf[s * PITCH : s * PITCH + LINES, :] = before_it
+        cf[at, :] = after_it
+        cjf[at, :] = jnp.dot(after_it.astype(BF), turn, preferred_element_type=F32)
 
     across = iota((LANES, LANES), 0) + iota((LANES, LANES), 1) >= LANES - 1
 
     def lag_line(line):
-        here = xjf[pl.ds(line, blocks, stride=LINES), :].astype(BF)
+        here = xjf[pl.ds(line, blocks, stride=PITCH), :].astype(BF)
         later = jnp.concatenate(
             [
-                cf[pl.ds(s * LINES + line, blocks, stride=LINES), :].astype(BF)
+                cf[pl.ds(s * PITCH + line, blocks, stride=PITCH), :].astype(BF)
                 for s in range(SHIFTS + 1)
             ],
             axis=1,
@@ -259,19 +225,18 @@
         for s in range(SHIFTS + 1):
             span = slice(s * LANES, (s + 1) * LANES)
             lhs[line, 0:blocks, span] = xf[
-                pl.ds((SHIFTS - s) * LINES + line, blocks, stride=LINES), :
+                pl.ds((SHIFTS - s) * PITCH + line, blocks, stride=PITCH), :
             ].astype(BF)
             lhs[line, blocks : 2 * blocks, span] = cjf[
-                pl.ds(s * LINES + line, blocks, stride=LINES), :
+                pl.ds(s * PITCH + line, blocks, stride=PITCH), :
             ].astype(BF)
 
     def before(step, carry):
-        for u in range(2):
-            lag_line(step * 2 + u)
-            windows(step * 2 + u)
+        for u in range(8):
+            lag_line(step * 8 + u)
         return carry
 
-    lax.fori_loop(0, LINES // 2, before, 0)
+    lax.fori_loop(0, LINES // 8, before, 0)
     scale = 1.0 / math.sqrt(2 * blocks * LANES)
     lag = jnp.concatenate(
         [
@@ -283,10 +248,51 @@
     lx_out[...] = jnp.where(tap_mask, lag, 0.0) * scale
     lag_swap = swap(lx_out, lx_in, lx_sem)
     lag_swap.start()
+    ins[4].wait()
+    arrived(rq_in, rq_sem)
+    asked = rq_in[...].reshape(chips, BANK_ROWS)
+    first = one_hot((asked == 1.0) | (asked == 3.0))
+    second = one_hot(asked >= 2.0)
+    owned[...] = jnp.concatenate([first, second], axis=0).astype(BF)
+
+    def pack_slots(values, out_ref):
+        for slot in range(SLOTS):
+            for s in range(SHIFTS):
+                stage[pl.ds(slot * SHIFTS + s, chips, stride=SLOTS * SHIFTS), :] = values[
+                    slot * chips : (slot + 1) * chips, s * LANES : (s + 1) * LANES
+                ]
+        out_ref[...] = stage[...].reshape(chips, SLOTS * SHIFTS, LANES).astype(BF)
+
+    def unpack_slots(in_ref):
+        stage[...] = in_ref[...].astype(F32).reshape(chips * SLOTS * SHIFTS, LANES)
+        return jnp.concatenate(
+            [
+                jnp.concatenate(
+                    [
+                        stage[pl.ds(slot * SHIFTS + s, chips, stride=SLOTS * SHIFTS), :]
+                        for s in range(SHIFTS)
+                    ],
+                    axis=1,
+                )
+                for slot in range(SLOTS)
+            ],
+            axis=0,
+        ).astype(BF)
+
+    pack_slots(jnp.dot(owned[...], bank[...], preferred_element_type=F32), fe_out)
+    scatter(fe_out, fe_in, fe_sem)
+
+    def prepare(step, carry):
+        for u in range(2):
+            windows(step * 2 + u)
+        return carry
+
     lag_swap.wait_recv()
     lag = (lx_out[...] + lx_in[...]).astype(BF)
     pack_slots(jnp.dot(pick_t, lag, preferred_element_type=F32), re_out)
     scatter(re_out, re_in, re_sem)
+    lax.fori_loop(0, LINES // 2, prepare, 0)
+
 
     arrived(fe_in, fe_sem)
     mine = jnp.dot(pick, unpack_slots(fe_in), preferred_element_type=F32)
@@ -314,34 +320,26 @@
         both = jnp.dot(
             lhs[line], jnp.concatenate(bands, axis=0), preferred_element_type=F32
         )
-        of[pl.ds(line, blocks, stride=LINES), :] = both[:blocks]
-        gf[pl.ds(line, blocks, stride=LINES), :] = both[blocks:]
+        of[pl.ds(line, blocks, stride=PITCH), :] = both[:blocks]
+        gf[pl.ds(line, blocks, stride=PITCH), :] = both[blocks:]
 
     def filters(half):
         def step_of(step, carry):
-            for u in range(2):
-                filter_line(half * 16 + step * 2 + u)
+            for u in range(16):
+                filter_line(half * 16 + step * 16 + u)
             return carry
 
-        lax.fori_loop(0, 8, step_of, 0)
-        copies = []
+        lax.fori_loop(0, 1, step_of, 0)
         at = slice(half * 16, half * 16 + 16)
         for q in range(blocks):
             span = slice(q * LANES, (q + 1) * LANES)
-            from_ = slice(q * LINES + half * 16, q * LINES + half * 16 + 16)
+            from_ = slice(q * PITCH + half * 16, q * PITCH + half * 16 + 16)
             fil[at, span] = of[from_, :].astype(BF)
             grad[at, span] = jnp.dot(
                 gf[from_, :].astype(BF), turn, preferred_element_type=F32
             ).astype(BF)
-        copies = [
-            pltpu.make_async_copy(fil.at[at], fil_hbm.at[at], out_sem.at[2 * half]),
-            pltpu.make_async_copy(grad.at[at], grad_hbm.at[at], out_sem.at[2 * half + 1]),
-        ]
-        for copy in copies:
-            copy.start()
-        return copies
-
-    outs = filters(0)
+
+    filters(0)
 
     arrived(re_in, re_sem)
     total = lax.dot_general(
@@ -353,11 +351,9 @@
     sum_swap = swap(gx_out, gx_in, gx_sem)
     sum_swap.start()
 
-    outs = outs + filters(1)
+    filters(1)
     sum_swap.wait_recv()
     bgrad[...] = bgrad[...] + gx_in[...]
-    outs.append(pltpu.make_async_copy(bgrad, bgrad_hbm, out_sem.at[4]))
-    outs[-1].start()
 
     pltpu.make_async_copy(halo, halo, halo_sem.at[0]).wait()
     departed(rq_out, rq_sem)
@@ -366,6 +362,16 @@
     lag_swap.wait_send()
     tap_swap.wait_send()
     sum_swap.wait_send()
+
+
+def finish(fil, grad, bgrad, fil_hbm, grad_hbm, bgrad_hbm, sem):
+    outs = [
+        pltpu.make_async_copy(fil, fil_hbm, sem.at[0]),
+        pltpu.make_async_copy(grad, grad_hbm, sem.at[1]),
+        pltpu.make_async_copy(bgrad, bgrad_hbm, sem.at[2]),
+    ]
+    for copy in outs:
+        copy.start()
     for copy in outs:
         copy.wait()
 
@@ -378,22 +384,22 @@
     vmem = pl.BlockSpec(memory_space=pltpu.VMEM)
     message = (chips, SLOTS * SHIFTS, LANES)
     pair = pltpu.SemaphoreType.DMA((2,))
-    return pl.pallas_call(
+    shapes = (
+        ((line_count, samples), BF),
+        ((line_count, samples), BF),
+        ((BANK_ROWS, TAPS // 2), F32),
+    )
+    results = pl.pallas_call(
         kernel,
-        out_shape=(
-            jax.ShapeDtypeStruct((line_count, samples), BF),
-            jax.ShapeDtypeStruct((line_count, samples), BF),
-            jax.ShapeDtypeStruct((BANK_ROWS, TAPS // 2), F32),
-        ),
-        in_specs=[any_, any_, any_, vmem, vmem],
-        out_specs=(any_, any_, any_),
+        out_shape=tuple(pltpu.VMEM(*shape) for shape in shapes),
+        in_specs=[any_] * 5,
+        out_specs=(vmem,) * 3,
         scratch_shapes=[
             pltpu.VMEM((line_count, samples), BF),
             pltpu.VMEM((line_count, samples), BF),
             pltpu.VMEM((BANK_ROWS, TAPS), BF),
-            pltpu.VMEM((line_count, samples), BF),
-            pltpu.VMEM((line_count, samples), BF),
-            pltpu.VMEM((BANK_ROWS, TAPS // 2), F32),
+            pltpu.VMEM((line_count,), jnp.int32),
+            pltpu.VMEM((line_count,), jnp.int32),
             pltpu.VMEM((line_count, TAPS), BF),
             pltpu.VMEM((chips, 1, LANES), F32),
             pltpu.VMEM((chips, 1, LANES), F32),
@@ -407,28 +413,34 @@
             pltpu.VMEM((line_count, TAPS), F32),
             pltpu.VMEM((BANK_ROWS, TAPS // 2), F32),
             pltpu.VMEM((BANK_ROWS, TAPS // 2), F32),
-            pltpu.VMEM(((blocks + SHIFTS) * line_count, LANES), F32),
-            pltpu.VMEM(((blocks + SHIFTS) * line_count, LANES), F32),
-            pltpu.VMEM(((blocks + SHIFTS) * line_count, LANES), F32),
-            pltpu.VMEM((blocks * line_count, LANES), F32),
+            pltpu.VMEM(((blocks + SHIFTS) * PITCH, LANES), F32),
+            pltpu.VMEM(((blocks + SHIFTS) * PITCH, LANES), F32),
+            pltpu.VMEM(((blocks + SHIFTS) * PITCH, LANES), F32),
+            pltpu.VMEM((blocks * PITCH, LANES), F32),
             pltpu.VMEM((line_count, 2 * blocks, TAPS + LANES), BF),
             pltpu.VMEM((SHIFTS, 8 * line_count, LANES), F32),
             pltpu.VMEM((SHIFTS * line_count, LANES), F32),
             pltpu.VMEM((chips * SLOTS * SHIFTS, LANES), F32),
             pltpu.VMEM((SLOTS * chips, BANK_ROWS), BF),
-            pltpu.VMEM((blocks * line_count, LANES), F32),
-            pltpu.VMEM((blocks * line_count, LANES), F32),
-            pltpu.SemaphoreType.DMA((3,)),
+            pltpu.VMEM((blocks * PITCH, LANES), F32),
+            pltpu.VMEM((blocks * PITCH, LANES), F32),
             pltpu.SemaphoreType.DMA((5,)),
             pair, pair, pair, pair, pair, pair, pair,
         ],
         compiler_params=pltpu.CompilerParams(
-            collective_id=0, has_side_effects=True, vmem_limit_bytes=48 * 1024 * 1024
+            collective_id=0, has_side_effects=True, vmem_limit_bytes=60 * 1024 * 1024
         ),
         cost_estimate=pl.CostEstimate(
             flops=6 * line_count * samples * TAPS, bytes_accessed=1 << 21, transcendentals=0
         ),
     )(signal, cotangent, bank, lengths, kernel_ids)
+    return pl.pallas_call(
+        finish,
+        out_shape=tuple(jax.ShapeDtypeStruct(*shape) for shape in shapes),
+        in_specs=[vmem] * 3,
+        out_specs=(any_,) * 3,
+        scratch_shapes=[pltpu.SemaphoreType.DMA((3,))],
+    )(*[pltpu.with_memory_space_constraint(r, pltpu.VMEM) for r in results])
 
 
 def solution(mesh):

time: 56.2 us -> 34.4 us (0.61)
  Pallas kernels: 49.2 us -> 33.7 us
  local copies, waits for them, and re-layouts: 6.17 us -> 0 us
    pallas_call x1 -> x2, Pallas kernels: 49.2 us -> 33.7 us  [the longest x1 32.8 us: body(): pl.pallas_call(kernel, out_shape=tuple((pltpu.VMEM(*shape) for shape in s...]
    unnamed x13 -> x0, local copies, waits for them, and re-layouts: 6.17 us -> none
where the time goes in v2:
time: 34.4 us; the launch traced here: 34.3 us
  Pallas kernels  33.7 us (98%)
  between operations  0.64 us (2%)
    pallas_call x1, Pallas kernels, body(): pl.pallas_call(kernel, out_shape=tuple((pltpu.VMEM(*shape) for shape in s...  32.8 us
    pallas_call x1, Pallas kernels, body(): pl.pallas_call(finish, out_shape=tuple((jax.ShapeDtypeStruct(*shape) for...  0.86 us

profile of v2, /device:TPU:1, one launch (start us, length us, event | category | flops | bytes accessed | tf_op | source)
XLA Modules:
  0.0 34.3 jit_solution(5953732896730467489)
XLA Ops:
  0.6 32.8 %shard_map.76 = (bf16[32,4096]{1,0:T(8,128)(2,1)S(1)}, bf16[32,4096]{1,0:T(8,128)(2,1)S(1)}, f32[128,256]{1,0:T(8,128)S(1)}) custom-call(bf16[32,4096]{1,0:T(8,128)(2,1)} %sig_hbm.1, bf16[32,4096]{1,0:T(8,128)(2,1)} %cot_hbm.1, bf16[128,512]{1,0:T(8,128)(2,1)} %bank_hbm.1, s32[32]{0:T(128)} %len_hbm.1, s32[32]{0:T(128)} %ids_hbm.1), custom_call_target="tpu_custom_call" | custom-call | flops 402653184 | bytes 2097152 | tf_op jit(solution)/shard_map/pallas_call | solution.py:392
  33.5 0.9 %shard_map.77 = (bf16[32,4096]{1,0:T(8,128)(2,1)}, bf16[32,4096]{1,0:T(8,128)(2,1)}, f32[128,256]{1,0:T(8,128)}) custom-call(bf16[32,4096]{1,0:T(8,128)(2,1)S(1)} %get-tuple-element.6.fil, bf16[32,4096]{1,0:T(8,128)(2,1)S(1)} %get-tuple-element.7.grad, f32[128,256]{1,0:T(8,128)S(1)} %get-tuple-element.8.bgrad), custom_call_target="tpu_custom_call" | custom-call | tf_op jit(solution)/shard_map/pallas_call | solution.py:437

commit v3 on v2

--- a/solution.py
+++ b/solution.py
@@ -15,8 +15,10 @@
 LANES = 128
 SHIFTS = TAPS // LANES
 SLOTS = 2
+ROWS = SLOTS * SHIFTS
 BANK_ROWS = 128
 PITCH = LINES + 1
+STEP = ROWS + 1
 
 
 def iota(shape, dim):
@@ -258,18 +260,20 @@
     def pack_slots(values, out_ref):
         for slot in range(SLOTS):
             for s in range(SHIFTS):
-                stage[pl.ds(slot * SHIFTS + s, chips, stride=SLOTS * SHIFTS), :] = values[
+                stage[pl.ds(slot * SHIFTS + s, chips, stride=STEP), :] = values[
                     slot * chips : (slot + 1) * chips, s * LANES : (s + 1) * LANES
                 ]
-        out_ref[...] = stage[...].reshape(chips, SLOTS * SHIFTS, LANES).astype(BF)
+        for i in range(chips):
+            out_ref[i] = stage[i * STEP : i * STEP + ROWS, :].astype(BF)
 
     def unpack_slots(in_ref):
-        stage[...] = in_ref[...].astype(F32).reshape(chips * SLOTS * SHIFTS, LANES)
+        for i in range(chips):
+            stage[i * STEP : i * STEP + ROWS, :] = in_ref[i].astype(F32)
         return jnp.concatenate(
             [
                 jnp.concatenate(
                     [
-                        stage[pl.ds(slot * SHIFTS + s, chips, stride=SLOTS * SHIFTS), :]
+                        stage[pl.ds(slot * SHIFTS + s, chips, stride=STEP), :]
                         for s in range(SHIFTS)
                     ],
                     axis=1,
@@ -297,12 +301,20 @@
     arrived(fe_in, fe_sem)
     mine = jnp.dot(pick, unpack_slots(fe_in), preferred_element_type=F32)
     kx_out[...] = jnp.where(tap_mask, mine, 0.0).astype(BF)
-    tap_swap = swap(kx_out, kx_in, kx_sem)
-    tap_swap.start()
-    tap_swap.wait_recv()
-    taps = kx_out[...].astype(F32) + kx_in[...].astype(F32)
-    for s in range(SHIFTS):
-        kf[s * LINES : (s + 1) * LINES, :] = taps[:, s * LANES : (s + 1) * LANES]
+    tap_swaps = []
+    for part in range(2):
+        at = pl.ds(part * (LINES // 2), LINES // 2)
+        tap_swaps.append(swap(kx_out.at[at], kx_in.at[at], kx_sem.at[part]))
+        tap_swaps[-1].start()
+
+    def settle(part):
+        tap_swaps[part].wait_recv()
+        at = slice(part * (LINES // 2), (part + 1) * (LINES // 2))
+        taps = kx_out[at, :].astype(F32) + kx_in[at, :].astype(F32)
+        for s in range(SHIFTS):
+            kf[s * LINES + at.start : s * LINES + at.stop, :] = taps[
+                :, s * LANES : (s + 1) * LANES
+            ]
 
     upper = iota((LANES, LANES), 1) >= iota((LANES, LANES), 0)
 
@@ -339,8 +351,6 @@
                 gf[from_, :].astype(BF), turn, preferred_element_type=F32
             ).astype(BF)
 
-    filters(0)
-
     arrived(re_in, re_sem)
     total = lax.dot_general(
         owned[...], unpack_slots(re_in), (((0,), (0,)), ((), ())), preferred_element_type=F32
@@ -351,6 +361,10 @@
     sum_swap = swap(gx_out, gx_in, gx_sem)
     sum_swap.start()
 
+    settle(0)
+    filters(0)
+    settle(1)
+
     filters(1)
     sum_swap.wait_recv()
     bgrad[...] = bgrad[...] + gx_in[...]
@@ -360,7 +374,8 @@
     departed(fe_out, fe_sem)
     departed(re_out, re_sem)
     lag_swap.wait_send()
-    tap_swap.wait_send()
+    for tap_swap in tap_swaps:
+        tap_swap.wait_send()
     sum_swap.wait_send()
 
 
@@ -420,12 +435,12 @@
             pltpu.VMEM((line_count, 2 * blocks, TAPS + LANES), BF),
             pltpu.VMEM((SHIFTS, 8 * line_count, LANES), F32),
             pltpu.VMEM((SHIFTS * line_count, LANES), F32),
-            pltpu.VMEM((chips * SLOTS * SHIFTS, LANES), F32),
+            pltpu.VMEM((chips * STEP, LANES), F32),
             pltpu.VMEM((SLOTS * chips, BANK_ROWS), BF),
             pltpu.VMEM((blocks * PITCH, LANES), F32),
             pltpu.VMEM((blocks * PITCH, LANES), F32),
             pltpu.SemaphoreType.DMA((5,)),
-            pair, pair, pair, pair, pair, pair, pair,
+            pair, pair, pair, pair, pltpu.SemaphoreType.DMA((2, 2)), pair, pair,
         ],
         compiler_params=pltpu.CompilerParams(
             collective_id=0, has_side_effects=True, vmem_limit_bytes=60 * 1024 * 1024

time: 34.4 us -> 34.4 us (level)
  no operation moved by 1% of the time
where the time goes in v3:
time: 34.4 us; the launch traced here: 34.3 us
  Pallas kernels  33.6 us (98%)
  between operations  0.64 us (2%)
    pallas_call x1, Pallas kernels, body(): pl.pallas_call(kernel, out_shape=tuple((pltpu.VMEM(*shape) for shape in s...  32.8 us
    pallas_call x1, Pallas kernels, body(): pl.pallas_call(finish, out_shape=tuple((jax.ShapeDtypeStruct(*shape) for...  0.86 us

profile of v3, /device:TPU:1, one launch (start us, length us, event | category | flops | bytes accessed | tf_op | source)
XLA Modules:
  0.0 34.3 jit_solution(5657607105138524123)
XLA Ops:
  0.6 32.8 %shard_map.76 = (bf16[32,4096]{1,0:T(8,128)(2,1)S(1)}, bf16[32,4096]{1,0:T(8,128)(2,1)S(1)}, f32[128,256]{1,0:T(8,128)S(1)}) custom-call(bf16[32,4096]{1,0:T(8,128)(2,1)} %sig_hbm.1, bf16[32,4096]{1,0:T(8,128)(2,1)} %cot_hbm.1, bf16[128,512]{1,0:T(8,128)(2,1)} %bank_hbm.1, s32[32]{0:T(128)} %len_hbm.1, s32[32]{0:T(128)} %ids_hbm.1), custom_call_target="tpu_custom_call" | custom-call | flops 402653184 | bytes 2097152 | tf_op jit(solution)/shard_map/pallas_call | solution.py:407
  33.4 0.9 %shard_map.77 = (bf16[32,4096]{1,0:T(8,128)(2,1)}, bf16[32,4096]{1,0:T(8,128)(2,1)}, f32[128,256]{1,0:T(8,128)}) custom-call(bf16[32,4096]{1,0:T(8,128)(2,1)S(1)} %get-tuple-element.6.fil, bf16[32,4096]{1,0:T(8,128)(2,1)S(1)} %get-tuple-element.7.grad, f32[128,256]{1,0:T(8,128)S(1)} %get-tuple-element.8.bgrad), custom_call_target="tpu_custom_call" | custom-call | tf_op jit(solution)/shard_map/pallas_call | solution.py:452
